TPU v7x, 256 devices: a whole 4x4x8 slice. The times are simulated.
256 devices in a mesh: seg: 16 (over y, x), ctx: 16 (over z, core).
Axes of the slice: x: 4, y: 4, z: 8, core: 2. Of those that a mesh axis runs over, the one named last changes fastest.
Arguments:
- queries: bfloat16 [393216, 1024], P(('seg', 'ctx')), may hold values from -6 to 6
- keys: bfloat16 [393216, 1024], P(('seg', 'ctx')), may hold values from -6 to 6
- values: bfloat16 [393216, 1024], P(('seg', 'ctx')), may hold values from -6 to 6
- log_decay: float32 [8, 393216], P(None, ('seg', 'ctx')), may hold values from -1 to 0, as said below
- gain: float32 [1024], replicated, may hold values from 0.1 to 1.9
Outputs:
- attended: bfloat16 [393216, 1024], P(('seg', 'ctx'))
Inputs may be any that keep to these rules, and one draw needn't show every extreme that they name: `log_decay`: every entry is negative.
All inputs are finite; a program needn't handle non-finite values.
Results may differ from a plain program's by a relative error of at most 0.0039.
Values sent between devices are 32-bit elements; how exact they have to be, the bound alone decides.
A program may use at most 320 MiB of HBM per device.

v0:
```python
import jax
import jax.numpy as jnp
from jax import lax
from jax.sharding import PartitionSpec as P

HEADS_PER_BATCH = 8
HD = 128
BLOCK = 512


def entering(x, axis, combine, identity):
    size, index = (lax.axis_size(axis), lax.axis_index(axis))
    everything = jax.tree.map(lambda part: lax.all_gather(part, axis), x)
    start = jax.tree.map(
        lambda part, zero: jnp.broadcast_to(jnp.asarray(zero, part.dtype), part.shape), x, identity
    )

    def turn(k, before):
        reached = k < index
        new = combine(before, jax.tree.map(lambda part: part[k], everything))
        return jax.tree.map(lambda a, b: jnp.where(reached, a, b), new, before)

    return lax.fori_loop(0, size, turn, start)


def broadcast(value, axis, source):
    kept = jnp.where(lax.axis_index(axis) == source, value, 0).astype(value.dtype)
    return lax.psum(kept, axis)


def block_step(state, queries, keys, values, decay):
    cum = jnp.cumsum(decay, axis=1)
    size = decay.shape[1]
    rows = lax.broadcasted_iota(jnp.int32, (size, size), 0)
    cols = lax.broadcasted_iota(jnp.int32, (size, size), 1)
    below = (cols <= rows)[None]
    scores = jnp.einsum("thd,shd->hts", queries, keys, preferred_element_type=jnp.float32)
    spread = jnp.where(below, cum[:, :, None] - cum[:, None, :], 0.0)
    weights = jnp.where(below, jnp.exp(spread), 0.0) * scores
    weights = weights.astype(jnp.bfloat16)
    inside = jnp.einsum("hts,shd->thd", weights, values, preferred_element_type=jnp.float32)
    scaled = queries.astype(jnp.float32) * jnp.exp(cum).T[:, :, None]
    inside = inside + jnp.einsum("thd,hde->the", scaled, state, precision=lax.Precision.HIGHEST)
    last = cum[:, -1]
    decayed_keys = (keys.astype(jnp.float32) * jnp.exp(last[:, None] - cum).T[:, :, None]).astype(
        jnp.bfloat16
    )
    added = jnp.einsum("shd,she->hde", decayed_keys, values, preferred_element_type=jnp.float32)
    state = jnp.exp(last)[:, None, None] * state + added
    return (state, inside)


def chain_join(earlier, later):
    return (jnp.exp(later[1])[:, None, None] * earlier[0] + later[0], earlier[1] + later[1])


def shards(queries, keys, values, log_decay, gain):
    tok_count = queries.shape[0]
    count = tok_count // BLOCK
    q_blocks = queries.reshape(count, BLOCK, HEADS_PER_BATCH, HD)
    k_blocks = keys.reshape(count, BLOCK, HEADS_PER_BATCH, HD)
    v_blocks = values.reshape(count, BLOCK, HEADS_PER_BATCH, HD)
    weakening_tiles = jnp.transpose(log_decay.reshape(HEADS_PER_BATCH, count, BLOCK), (1, 0, 2))

    def step(state, items):
        return block_step(state, items[0], items[1], items[2], items[3])

    start = jnp.zeros((HEADS_PER_BATCH, HD, HD), jnp.float32)
    own_state, inside = lax.scan(step, start, (q_blocks, k_blocks, v_blocks, weakening_tiles))
    inside = inside.reshape(tok_count, HEADS_PER_BATCH, HD)
    through = jnp.cumsum(log_decay, axis=1)
    own = (own_state, through[:, -1])
    empty = (
        jnp.zeros((HEADS_PER_BATCH, HD, HD), jnp.float32),
        jnp.zeros((HEADS_PER_BATCH,), jnp.float32),
    )
    within = entering(own, "ctx", chain_join, empty)
    whole = chain_join(within, own)
    total = (
        broadcast(whole[0], "ctx", lax.axis_size("ctx") - 1),
        broadcast(whole[1], "ctx", lax.axis_size("ctx") - 1),
    )
    before = entering(total, "seg", chain_join, empty)
    carry = chain_join(before, within)[0]
    scaled = (
        queries.reshape(tok_count, HEADS_PER_BATCH, HD).astype(jnp.float32)
        * jnp.exp(through).T[:, :, None]
    )
    heads_out = inside + jnp.einsum("thd,hde->the", scaled, carry, precision=lax.Precision.HIGHEST)
    scale = lax.rsqrt(jnp.mean(heads_out * heads_out, axis=-1, keepdims=True) + 1e-06)
    normed = heads_out * scale * gain.reshape(HEADS_PER_BATCH, HD)
    return normed.astype(jnp.bfloat16).reshape(tok_count, HEADS_PER_BATCH * HD)


def solution(mesh):
    in_specs = (
        P(("seg", "ctx"), None),
        P(("seg", "ctx"), None),
        P(("seg", "ctx"), None),
        P(None, ("seg", "ctx")),
        P(),
    )
    out_specs = P(("seg", "ctx"), None)
    return jax.shard_map(shards, mesh=mesh, in_specs=in_specs, out_specs=out_specs, check_vma=False)
```

profile of v0, /device:TPU:9, one launch (start us, length us, event | category | flops | bytes accessed | tf_op | source)
XLA Modules:
  0.0 396.8 jit_solution(16160947159411998315)
XLA Ops:
  6.5 4.6 %copy.75 = bf16[192,8,8,128]{3,2,1,0:T(8,128)(2,1)} copy(bf16[192,8,8,128]{3,1,2,0:T(8,128)(2,1)} %bitcast.131) | data formatting | bytes 6291456
  11.1 2.5 copy.76
  13.6 2.5 copy.77
  16.1 73.7 %while.43 = (s32[]{:T(128)}, f32[8,128,128]{2,1,0:T(8,128)}, f32[3,512,8,128]{3,2,1,0:T(8,128)}, f32[3,8,512]{2,1,0:T(8,128)S(1)}, bf16[3,512,8,128]{3,2,1,0:T(8...) while((s32[]{:T(128)}, f32[8,128,128]{2,1,0:T(8,128)}, ...), condition=%wide.region_3.4_spmd.clone, body=%wide.region_0.3_spmd.clone.sunk | while | flops 2028212352 | bytes 37946664 | solution.py:69
  17.6 1.3 constant_dynamic-slice_fusion.6
  19.0 2.1 constant_dynamic-slice_fusion.7
  21.0 5.2 %fusion.35 = f32[8,128,512]{2,1,0:T(8,128)} fusion(f32[8,512]{1,0:T(8,128)S(1)} %get-tuple-element.511, pred[512,512]{1,0:T(8,128)(4,1)S(1)} %iota_compare_fusion.2, bf16[1,512,8,128]{3,2,1,0:T(8,128)(2,1)S(1)} %constant_dynamic-slice_fusion.6, bf16[1,512,8,128]{3,2,1,0:T(8,128)(2,1)S(1)} %get-tuple-element.512, ...), kind=kOutput, calls=%fused_computation.10.clone.1 | convolution fusion | flops 1084227584 | bytes 5521408 | tf_op jit(solution)/shard_map/while/body/eval_jaxpr/hts,shd->thd/dot_general | solution.py:41
  26.3 5.4 %fusion.36 = f32[1,512,8,128]{1,3,2,0:T(8,128)S(1)} fusion(f32[8,128,512]{2,1,0:T(8,128)} %fusion.35, f32[512,8]{0,1:T(8,128)S(1)} %get-tuple-element.514, bf16[1,512,8,128]{3,2,1,0:T(8,128)(2,1)S(1)} %get-tuple-element.513, f32[8,128,128]{2,1,0:T(8,128)} %get-tuple-element.539, pred[]{:T(512)S(6)} %compare.9), kind=kOutput, calls=%fused_computation.14.clone.1 | convolution fusion | flops 807010304 | bytes 5783553 | tf_op jit(solution)/shard_map/while/body/eval_jaxpr/thd,hde->the/dot_general | solution.py:43
  31.9 3.7 convolution_add_fusion.2
  35.6 1.8 copy.117
  37.5 3.1 constant_dynamic-update-slice_fusion.2
  42.1 1.3 constant_dynamic-slice_fusion.6
  43.4 2.1 constant_dynamic-slice_fusion.7
  45.5 5.2 %fusion.35 = f32[8,128,512]{2,1,0:T(8,128)} fusion(f32[8,512]{1,0:T(8,128)S(1)} %get-tuple-element.511, pred[512,512]{1,0:T(8,128)(4,1)S(1)} %iota_compare_fusion.2, bf16[1,512,8,128]{3,2,1,0:T(8,128)(2,1)S(1)} %constant_dynamic-slice_fusion.6, bf16[1,512,8,128]{3,2,1,0:T(8,128)(2,1)S(1)} %get-tuple-element.512, ...), kind=kOutput, calls=%fused_computation.10.clone.1 | convolution fusion | flops 1084227584 | bytes 5521408 | tf_op jit(solution)/shard_map/while/body/eval_jaxpr/hts,shd->thd/dot_general | solution.py:41
  50.7 5.5 %fusion.36 = f32[1,512,8,128]{1,3,2,0:T(8,128)S(1)} fusion(f32[8,128,512]{2,1,0:T(8,128)} %fusion.35, f32[512,8]{0,1:T(8,128)S(1)} %get-tuple-element.514, bf16[1,512,8,128]{3,2,1,0:T(8,128)(2,1)S(1)} %get-tuple-element.513, f32[8,128,128]{2,1,0:T(8,128)} %get-tuple-element.539, pred[]{:T(512)S(6)} %compare.9), kind=kOutput, calls=%fused_computation.14.clone.1 | convolution fusion | flops 807010304 | bytes 5783553 | tf_op jit(solution)/shard_map/while/body/eval_jaxpr/thd,hde->the/dot_general | solution.py:43
  56.5 3.8 convolution_add_fusion.2
  60.3 1.8 copy.117
  62.2 3.0 constant_dynamic-update-slice_fusion.2
  66.7 1.3 constant_dynamic-slice_fusion.6
  68.0 2.1 constant_dynamic-slice_fusion.7
  70.1 5.2 %fusion.35 = f32[8,128,512]{2,1,0:T(8,128)} fusion(f32[8,512]{1,0:T(8,128)S(1)} %get-tuple-element.511, pred[512,512]{1,0:T(8,128)(4,1)S(1)} %iota_compare_fusion.2, bf16[1,512,8,128]{3,2,1,0:T(8,128)(2,1)S(1)} %constant_dynamic-slice_fusion.6, bf16[1,512,8,128]{3,2,1,0:T(8,128)(2,1)S(1)} %get-tuple-element.512, ...), kind=kOutput, calls=%fused_computation.10.clone.1 | convolution fusion | flops 1084227584 | bytes 5521408 | tf_op jit(solution)/shard_map/while/body/eval_jaxpr/hts,shd->thd/dot_general | solution.py:41
  75.3 5.5 %fusion.36 = f32[1,512,8,128]{1,3,2,0:T(8,128)S(1)} fusion(f32[8,128,512]{2,1,0:T(8,128)} %fusion.35, f32[512,8]{0,1:T(8,128)S(1)} %get-tuple-element.514, bf16[1,512,8,128]{3,2,1,0:T(8,128)(2,1)S(1)} %get-tuple-element.513, f32[8,128,128]{2,1,0:T(8,128)} %get-tuple-element.539, pred[]{:T(512)S(6)} %compare.9), kind=kOutput, calls=%fused_computation.14.clone.1 | convolution fusion | flops 807010304 | bytes 5783553 | tf_op jit(solution)/shard_map/while/body/eval_jaxpr/thd,hde->the/dot_general | solution.py:43
  81.1 3.8 convolution_add_fusion.2
  84.9 1.8 copy.117
  86.8 3.1 constant_dynamic-update-slice_fusion.2
  90.0 2.3 reduce-window.16
  94.5 27.5 %all-reduce = f32[128]{0:T(128)S(1)} all-reduce(f32[128]{0:T(128)S(1)} %dynamic-update-slice), channel_id=2, replica_groups=mesh['seg'=16,'ctx'=16] {'ctx'}, use_global_device_ids=true, to_apply=%add | all-reduce | flops 128 | bytes 1024
  122.1 27.4 %all-gather.8.cloned.1.call-done = f32[128,128,128]{2,1,0:T(8,128)} async-done(((f32[8,128,128]{2,1,0:T(8,128)}), f32[128,128,128]{2,1,0:T(8,128)}) %all-gather.8.cloned.1.call-update) | async-done | bytes 8388624 | tf_op jit(solution)/shard_map/all_gather | solution.py:13
  149.5 19.5 %while.44 = (s32[]{:T(128)}, f32[8,128,128]{2,1,0:T(8,128)S(1)}, f32[8]{0:T(128)S(1)}, s32[]{:T(128)}, f32[16,8]{1,0:T(8,128)S(1)}, /*index=5*/f32[16,8,128,128]{3,2,1,0:T(8,128)}, s32[]{:T(128)}, s32[]{:T(128)}) while((s32[]{:T(128)}, f32[8,128,128]{2,1,0:T(8,128)S(1)}, f32[8]{0:T(128)S(1)}, s32[]{:T(128)}, ...), condition=%wide.region_7.8_spmd.clone, body=%wide.region_6.7_spmd.clone.sunk | while | flops 524316 | bytes 1573147 | solution.py:23
  150.7 1.2 fusion.37
  151.9 1.2 fusion.37
  153.2 1.2 fusion.37
  154.4 1.2 fusion.37
  155.6 1.2 fusion.37
  156.8 1.2 fusion.37
  158.1 1.2 fusion.37
  159.3 1.2 fusion.37
  160.5 1.2 fusion.37
  161.7 1.2 fusion.37
  162.9 1.2 fusion.37
  164.2 1.2 fusion.37
  165.4 1.2 fusion.37
  166.6 1.2 fusion.37
  167.8 1.2 fusion.37
  170.0 107.8 %all-reduce.3.cloned.1.call-done = f32[1,8,128,128]{3,2,1,0:T(8,128)} async-done(((f32[1,8,128,128]{3,2,1,0:T(8,128)}), f32[1,8,128,128]{3,2,1,0:T(8,128)}) %all-reduce.3.cloned.1.call-update) | async-done | bytes 524304 | tf_op jit(solution)/shard_map/psum | solution.py:28
  277.9 6.7 %copy.59 = f32[1536,8,128]{0,2,1:T(8,128)} copy(f32[1536,8,128]{2,1,0:T(8,128)} %bitcast.130) | data formatting | bytes 12582912 | tf_op jit(solution)/shard_map/reshape | solution.py:70
  284.6 24.0 %psum.14 = f32[1,8]{1,0:T(1,128)S(1)} all-reduce(f32[1,8]{1,0:T(1,128)S(1)} %get-tuple-element.401), channel_id=1, replica_groups=mesh['seg'=16,'ctx'=16] {'ctx'}, use_global_device_ids=true, to_apply=%region_9.10 | all-reduce | flops 8 | bytes 64 | tf_op jit(solution)/shard_map/psum | solution.py:28
  308.6 17.1 %all-gather.2 = f32[16,1,8]{2,1,0:T(1,128)S(1)} all-gather(f32[1,1,8]{2,1,0:T(1,128)S(1)} %bitcast.139), channel_id=1, replica_groups=mesh['seg'=16,'ctx'=16] {'seg'}, dimensions={0}, use_global_device_ids=true | all-gather | bytes 544 | tf_op jit(solution)/shard_map/all_gather | solution.py:13
  325.6 31.2 %all-gather.6.cloned.1.call-done = f32[16,8,128,128]{3,2,1,0:T(8,128)} async-done(((f32[1,8,128,128]{3,2,1,0:T(8,128)}), f32[16,8,128,128]{3,2,1,0:T(8,128)}) %all-gather.6.cloned.1.call-update) | async-done | bytes 8388624 | tf_op jit(solution)/shard_map/all_gather | solution.py:13
  356.8 19.5 %while.45 = (s32[]{:T(128)}, f32[8,128,128]{2,1,0:T(8,128)S(1)}, s32[]{:T(128)}, f32[16,8]{1,0:T(8,128)S(1)}, f32[16,8,128,128]{3,2,1,0:T(8,128)}, /*index=5*/s32[]{:T(128)}, s32[]{:T(128)}) while((s32[]{:T(128)}, f32[8,128,128]{2,1,0:T(8,128)S(1)}, s32[]{:T(128)}, f32[16,8]{1,0:T(8,128)S(1)}, f32[16,8,128,128]{3,2,1,0:T(8,128)}, ...), condition=%wide.region_11.12_spmd.clone, body=%wide.region_10.11_spmd.clone.sunk | while | flops 524292 | bytes 1573073 | solution.py:23
  356.8 1.2 fusion.38
  358.0 1.2 fusion.38
  359.2 1.2 fusion.38
  360.5 1.2 fusion.38
  361.7 1.2 fusion.38
  362.9 1.2 fusion.38
  364.1 1.2 fusion.38
  370.2 1.2 fusion.38
  371.4 1.2 fusion.38
  372.6 1.2 fusion.38
  373.9 1.2 fusion.38
  375.1 1.2 fusion.38
  376.3 10.4 %multiply_reduce_fusion = (f32[1536,8]{0,1:T(8,128)S(1)}, f32[1536,8,128]{0,2,1:T(8,128)S(1)}) fusion(f32[1536,8,128]{0,2,1:T(8,128)} %copy.59, f32[1536,8]{0,1:T(8,128)S(1)} %get-tuple-element.394, f32[8,128,128]{2,1,0:T(8,128)S(1)} %get-tuple-element.250, f32[8,128,128]{2,1,0:T(8,128)S(1)} %get-tuple-element.251, f32[8]{0:T(128)S(1)} %get-tuple-element.400, ...), kind=kOutput, calls=%fused_computation.47 | convolution fusion | flops 2424033280 | bytes 16875552 | tf_op jit(solution)/shard_map/thd,hde->the/dot_general | solution.py:89
  387.4 2.9 copy.60
  (116 shorter events, 15.1 us)
Async XLA Ops:
  6.5 4.6 %copy-start.4 = (bf16[1536,1024]{1,0:T(8,128)(2,1)S(1)}, bf16[1536,1024]{1,0:T(8,128)(2,1)}, u32[]{:S(2)}) copy-start(bf16[1536,1024]{1,0:T(8,128)(2,1)} %param.13) | copy-start | bytes 9437188
  6.5 143.0 %all-gather.8.cloned.1.call-start = ((), (), s32[]{:S(2)}) async-start(), calls=%async_computation.2 | async-start | bytes 8912896 | tf_op jit(solution)/shard_map/all_gather | solution.py:13
  6.5 7.1 %copy-start.3 = (bf16[1536,1024]{1,0:T(8,128)(2,1)S(1)}, bf16[1536,1024]{1,0:T(8,128)(2,1)}, u32[]{:S(2)}) copy-start(bf16[1536,1024]{1,0:T(8,128)(2,1)} %param.11) | copy-start | bytes 9437188
  11.1 5.0 %copy-start.5 = (f32[8,1536]{1,0:T(8,128)S(1)}, f32[8,1536]{1,0:T(8,128)}, u32[]{:S(2)}) copy-start(f32[8,1536]{1,0:T(8,128)} %param.14) | copy-start | bytes 147460
  16.1 76.5 %copy-start.7 = (u32[256]{0:T(256)S(1)}, u32[256]{0:T(256)}, u32[]{:S(2)}) copy-start(u32[256]{0:T(256)} %constant.89) | copy-start | bytes 3076
  18.9 7.3 %copy-start.1 = (bf16[1,512,8,128]{3,2,1,0:T(8,128)(2,1)}, bf16[1,512,8,128]{3,2,1,0:T(8,128)(2,1)S(1)}, u32[]{:S(2)}) copy-start(bf16[1,512,8,128]{3,2,1,0:T(8,128)(2,1)S(1)} %constant_dynamic-slice_fusion.6) | copy-start | bytes 3145732 | tf_op jit(solution)/shard_map/while
  21.0 5.3 %copy-start = (bf16[1,512,8,128]{3,2,1,0:T(8,128)(2,1)}, bf16[1,512,8,128]{3,2,1,0:T(8,128)(2,1)S(1)}, u32[]{:S(2)}) copy-start(bf16[1,512,8,128]{3,2,1,0:T(8,128)(2,1)S(1)} %get-tuple-element.512) | copy-start | bytes 3145732 | tf_op jit(solution)/shard_map/while
  43.4 7.3 %copy-start.1 = (bf16[1,512,8,128]{3,2,1,0:T(8,128)(2,1)}, bf16[1,512,8,128]{3,2,1,0:T(8,128)(2,1)S(1)}, u32[]{:S(2)}) copy-start(bf16[1,512,8,128]{3,2,1,0:T(8,128)(2,1)S(1)} %constant_dynamic-slice_fusion.6) | copy-start | bytes 3145732 | tf_op jit(solution)/shard_map/while
  45.5 5.3 %copy-start = (bf16[1,512,8,128]{3,2,1,0:T(8,128)(2,1)}, bf16[1,512,8,128]{3,2,1,0:T(8,128)(2,1)S(1)}, u32[]{:S(2)}) copy-start(bf16[1,512,8,128]{3,2,1,0:T(8,128)(2,1)S(1)} %get-tuple-element.512) | copy-start | bytes 3145732 | tf_op jit(solution)/shard_map/while
  68.0 7.3 %copy-start.1 = (bf16[1,512,8,128]{3,2,1,0:T(8,128)(2,1)}, bf16[1,512,8,128]{3,2,1,0:T(8,128)(2,1)S(1)}, u32[]{:S(2)}) copy-start(bf16[1,512,8,128]{3,2,1,0:T(8,128)(2,1)S(1)} %constant_dynamic-slice_fusion.6) | copy-start | bytes 3145732 | tf_op jit(solution)/shard_map/while
  70.1 5.3 %copy-start = (bf16[1,512,8,128]{3,2,1,0:T(8,128)(2,1)}, bf16[1,512,8,128]{3,2,1,0:T(8,128)(2,1)S(1)}, u32[]{:S(2)}) copy-start(bf16[1,512,8,128]{3,2,1,0:T(8,128)(2,1)S(1)} %get-tuple-element.512) | copy-start | bytes 3145732 | tf_op jit(solution)/shard_map/while
  89.8 79.2 %copy-start.2 = (f32[8,128,128]{2,1,0:T(8,128)S(1)}, f32[8,128,128]{2,1,0:T(8,128)}, u32[]{:S(2)}) copy-start(f32[8,128,128]{2,1,0:T(8,128)} %get-tuple-element.248) | copy-start | bytes 1572868
  89.9 188.0 %all-reduce.3.cloned.1.call-start = ((), (), s32[]{:S(2)}) async-start(), calls=%async_computation | async-start | bytes 1048576 | tf_op jit(solution)/shard_map/psum | solution.py:28
  170.0 186.8 %all-gather.6.cloned.1.call-start = ((), (), s32[]{:S(2)}) async-start(), calls=%async_computation.1 | async-start | bytes 8912896 | tf_op jit(solution)/shard_map/all_gather | solution.py:13
  376.3 10.4 %copy-start.6 = (f32[1024]{0:T(1024)S(1)}, f32[1024]{0:T(1024)}, u32[]{:S(2)}) copy-start(f32[1024]{0:T(1024)} %param.15) | copy-start | bytes 12292
Sparse Core Ops, SparseCore 0:
  90.0 59.4 all-gather.7
  170.1 107.6 all-reduce.2
  280.6 76.1 all-gather.5
where the time goes:
time: 400 us; the launch traced here: 397 us
  waiting for transfers between devices  166 us (42%)
  blocking collectives  68.6 us (17%)
  matrix products  53.8 us (13%)
  local copies, waits for them, and re-layouts  46.6 us (12%)
  other arithmetic  46.3 us (12%)
  between operations  13.9 us (3%)
    psum x1, waiting for transfers between devices, broadcast(): return lax.psum(kept, axis)  108 us
    all_gather x2, waiting for transfers between devices, entering(): everything = jax.tree.map(lambda part: lax.all_gather(part, axis), x)  58.6 us
    select_n x48, other arithmetic, turn(): return jax.tree.map(lambda a, b: jnp.where(reached, a, b), new, before)  37.9 us
    unnamed x1, blocking collectives  27.5 us
    psum x1, blocking collectives, broadcast(): return lax.psum(kept, axis)  24 us
    all_gather x1, blocking collectives, entering(): everything = jax.tree.map(lambda part: lax.all_gather(part, axis), x)  17.1 us
    dot_general x3, matrix products, block_step(): jnp.einsum('thd,hde->the', scaled, state, precision=lax.Precision.HIGHEST)  16.3 us
    dot_general x3, matrix products, block_step(): jnp.einsum('hts,shd->thd', weights, values, preferred_element_type=jnp.fl...  15.7 us
  transfers between devices with their start and end apart: 3, of which 3 were waited for; matrix products, arithmetic and copies ran while one was open for 3% of the time, Pallas kernels for 0%

commit v1 on v0

v1 whole, which is shorter than its diff:
```python
import jax
import jax.numpy as jnp
from jax import lax
from jax.experimental import pallas as pl
from jax.experimental.pallas import tpu as pltpu
from jax.sharding import PartitionSpec as P

HEADS = 8
HD = 128
BLOCK = 512
TILE = 128
NY, NX, NZ = 4, 4, 8
HALF = HD // 2
SLAB = HALF + 8
MSG = HD + 8
MESH = pl.DeviceIdType.MESH
F32, BF16 = jnp.float32, jnp.bfloat16
SPLIT = (5, 1, 1, 1)


def order(i):
    return 4 + ((i + 1) // 2) * (1 - 2 * (i % 2))


def kernel(
    q_hbm, k_hbm, v_hbm, ld_hbm, gain_hbm, out_hbm,
    q_s, k_s, v_s, ld_s, gain_s, rows_s, cols_s, e_s, sblk_s, y_s, o_s,
    msg_s, peer_s, zs_s, zr_s, w_s, gp_s, xs_s, xr_s, ys_s, yr_s, cs_s, carry_s,
    q_sem, k_sem, v_sem, o_sem, small_sem,
    core_ss, core_rs, z_ss, z_rs, x_ss, x_rs, y_ss, y_rs, b_ss, b_rs, f_ss, f_rs,
):
    seg, ctx = lax.axis_index("seg"), lax.axis_index("ctx")
    y, x = seg // NX, seg % NX
    z, c = ctx // 2, ctx % 2
    tokens = k_s.shape[1]
    blocks = tokens // BLOCK
    tiles = BLOCK // TILE

    def head_of(i):
        return (z + order(i)) % NZ

    def columns(h):
        return pl.ds(pl.multiple_of(h * HD, HD), HD)

    def at_z(other):
        return (seg, other * 2 + c)

    def at_x(other):
        return (y * NX + other, ctx)

    def at_y(other):
        return (other * NX + x, ctx)

    partner = (seg, z * 2 + (1 - c))

    barrier = pltpu.get_barrier_semaphore()

    def signal(device):
        pl.semaphore_signal(barrier, inc=1, device_id=device, device_id_type=MESH)

    ld_copy = pltpu.make_async_copy(ld_hbm, ld_s, small_sem.at[0])
    gain_copy = pltpu.make_async_copy(gain_hbm, gain_s, small_sem.at[1])
    ld_copy.start()

    def load(hbm, vmem, sem, h):
        return pltpu.make_async_copy(hbm.at[:, columns(h)], vmem.at[h], sem.at[h])

    def start_kv(i, _):
        h = head_of(i)
        load(k_hbm, k_s, k_sem, h).start()
        load(v_hbm, v_s, v_sem, h).start()
        return 0

    lax.fori_loop(0, HEADS, start_kv, 0)
    gain_copy.start()

    def start_q(h, _):
        load(q_hbm, q_s, q_sem, h).start()
        return 0

    lax.fori_loop(0, HEADS, start_q, 0)
    signal(partner)
    for d in range(1, NZ):
        signal(at_z((z + d) % NZ))
    for d in range(1, NX):
        signal(at_x((x + d) % NX))
    for d in range(1, NY):
        signal(at_y((y + d) % NY))

    ld_copy.wait()
    count = tokens // TILE
    stacked = jnp.concatenate([ld_s[:, j * TILE : (j + 1) * TILE] for j in range(count)], axis=0)
    rows = lax.broadcasted_iota(jnp.int32, (TILE, TILE), 0)
    cols = lax.broadcasted_iota(jnp.int32, (TILE, TILE), 1)
    upto = (rows <= cols).astype(F32)
    within = jnp.dot(stacked, upto, precision=lax.Precision.HIGHEST, preferred_element_type=F32)
    within = [within[j * HEADS : (j + 1) * HEADS] for j in range(count)]
    col_c, col_r = [], []
    total = jnp.zeros((HEADS, 1), F32)
    for b in range(blocks):
        start = [jnp.zeros((HEADS, 1), F32)]
        cum = []
        for a in range(tiles):
            w = within[b * tiles + a]
            cum.append(w + start[a])
            start.append(start[a] + w[:, TILE - 1 : TILE])
            col_r.append(jnp.exp(w))
        last = start[tiles]
        col_c += cum
        for a in range(tiles):
            place = slice((b * tiles + a) * TILE, (b * tiles + a + 1) * TILE)
            rows_s[:, 0, place] = cum[a]
            rows_s[:, 4, place] = jnp.exp(last - cum[a])
            for m in range(a + 1, tiles):
                rows_s[:, m, place] = jnp.exp(start[m] - cum[a])
        e_s[:, b, :] = jnp.broadcast_to(jnp.exp(last), (HEADS, HD))
        total = total + last
    e_s[:, blocks, :] = jnp.broadcast_to(jnp.exp(total), (HEADS, HD))
    blank = jnp.zeros((TILE - count * HEADS, TILE), F32)
    cols_s[0] = jnp.transpose(jnp.concatenate(col_c + [blank], axis=0))
    cols_s[1] = jnp.transpose(jnp.concatenate(col_r + [blank], axis=0))
    cols_s[2] = jnp.exp(cols_s[0])

    def to_partner(h):
        return pltpu.make_async_remote_copy(
            src_ref=msg_s.at[h], dst_ref=peer_s.at[h], send_sem=core_ss.at[h], recv_sem=core_rs.at[h],
            device_id=partner, device_id_type=MESH,
        )

    def to_owner(h):
        return pltpu.make_async_remote_copy(
            src_ref=zs_s.at[h], dst_ref=zr_s.at[z], send_sem=z_ss.at[h], recv_sem=z_rs.at[z],
            device_id=at_z(h), device_id_type=MESH,
        )

    def from_shard(other):
        return pltpu.make_async_remote_copy(
            src_ref=zs_s.at[other], dst_ref=zr_s.at[other], send_sem=z_ss.at[other], recv_sem=z_rs.at[other],
            device_id=at_z(other), device_id_type=MESH,
        )

    def own_state(i):
        h = head_of(i)
        load(k_hbm, k_s, k_sem, h).wait()
        load(v_hbm, v_s, v_sem, h).wait()
        state = None
        for b in range(blocks):
            place = slice(b * BLOCK, (b + 1) * BLOCK)
            turned = jnp.transpose(k_s[h, place, :]).astype(F32)
            decayed = (turned * rows_s[h, 4:5, place]).astype(BF16)
            added = jnp.dot(decayed, v_s[h, place, :], preferred_element_type=F32)
            if b:
                sblk_s[h, b - 1] = state
                state = e_s[h, b : b + 1, :] * state + added
            else:
                state = added
        msg_s[h, 0:8, :] = jnp.broadcast_to(e_s[h, blocks : blocks + 1, :], (8, HD))
        msg_s[h, 8:MSG, :] = state

    def pair_state(i):
        h = head_of(i)
        to_partner(h).wait_recv()
        mine, other = msg_s[h, 0:8, :], peer_s[h, 0:8, :]
        half = pl.ds(pl.multiple_of(8 + c * HALF, 8), HALF)
        first = c == 0
        scale_mine = jnp.where(first, other, 1.0)[0:1]
        scale_other = jnp.where(first, 1.0, mine)[0:1]
        joined = scale_mine * msg_s[h, half, :] + scale_other * peer_s[h, half, :]
        zs_s[h, 0:8, :] = mine * other
        zs_s[h, 8:SLAB, :] = joined

        @pl.when(h != z)
        def _():
            to_owner(h).start()

        @pl.when(h == z)
        def _():
            zr_s[z, 0:8, :] = mine * other
            zr_s[z, 8:SLAB, :] = joined

    own_state(0)
    pl.semaphore_wait(barrier, 1 + (NZ - 1) + (NX - 1) + (NY - 1))
    to_partner(head_of(0)).start()
    own_state(1)
    to_partner(head_of(1)).start()

    def states(i, _):
        own_state(i)
        to_partner(head_of(i)).start()
        pair_state(i - 2)
        return 0

    lax.fori_loop(2, HEADS, states, 0)

    below = cols <= rows

    def attend(h, _):
        load(q_hbm, q_s, q_sem, h).wait()
        shift = (HD - h) % HD
        col_c = pltpu.roll(cols_s[0], shift, 1)
        col_r = pltpu.roll(cols_s[1], shift, 1)
        for b in range(blocks):
            for a in range(tiles):
                j = b * tiles + a
                here = slice(j * TILE, (j + 1) * TILE)
                seen = slice(b * BLOCK, (j + 1) * TILE)
                before = slice(b * BLOCK, j * TILE)
                scores = lax.dot_general(
                    q_s[h, here, :], k_s[h, seen, :], (((1,), (1,)), ((), ())), preferred_element_type=F32
                )
                spread = col_c[:, j * HEADS : j * HEADS + 1] - rows_s[h, 0:1, here]
                decay = jnp.where(below, jnp.exp(jnp.minimum(spread, 0.0)), 0.0)
                weights = (scores[:, a * TILE :] * decay).astype(BF16)
                if a:
                    fade = col_r[:, j * HEADS : j * HEADS + 1] * rows_s[h, a : a + 1, before]
                    weights = jnp.concatenate([(scores[:, : a * TILE] * fade).astype(BF16), weights], axis=1)
                y_s[h, here, :] = jnp.dot(weights, v_s[h, seen, :], preferred_element_type=F32)
        return 0

    pair_state(HEADS - 2)
    pair_state(HEADS - 1)
    marks = [0]
    for n in SPLIT:
        marks.append(marks[-1] + n)
    lax.fori_loop(marks[0], marks[1], attend, 0)

    def arrived(i, _):
        from_shard(head_of(i)).wait_recv()
        return 0

    lax.fori_loop(0, NZ - 1, arrived, 0)

    def fold(n, held):
        state, decay = held
        w_s[n] = state
        gp_s[n] = decay
        g = zr_s[n, 0:8, :]
        return (g[0:1] * state + zr_s[n, 8:SLAB, :], decay * g)

    empty = (jnp.zeros((HALF, HD), F32), jnp.ones((8, HD), F32))
    state, decay = lax.fori_loop(0, NZ, fold, empty)

    def exchange(state, decay, buf, got, ss, rs, me, size, at):
        buf[0:8, :] = decay
        buf[8:SLAB, :] = state
        got[me, 0:8, :] = decay
        got[me, 8:SLAB, :] = state

        def copy(d, sending):
            other = (me + d) % size if sending else (me + size - d) % size
            return pltpu.make_async_remote_copy(
                src_ref=buf, dst_ref=got.at[me if sending else other], send_sem=ss.at[d - 1], recv_sem=rs.at[d - 1],
                device_id=at(other), device_id_type=MESH,
            )

        for d in range(1, size):
            copy(d, True).start()
        return copy

    def collect(copy, got, me, size):
        for d in range(1, size):
            copy(d, False).wait_recv()
        state, decay = empty
        before, faded = empty
        for n in range(size):
            mine = me == n
            before, faded = jnp.where(mine, state, before), jnp.where(mine, decay, faded)
            g = got[n, 0:8, :]
            state, decay = g[0:1] * state + got[n, 8:SLAB, :], decay * g
        return before, faded, state, decay

    copy_x = exchange(state, decay, xs_s, xr_s, x_ss, x_rs, x, NX, at_x)
    lax.fori_loop(marks[1], marks[2], attend, 0)
    before_x, faded_x, state, decay = collect(copy_x, xr_s, x, NX)
    copy_y = exchange(state, decay, ys_s, yr_s, y_ss, y_rs, y, NY, at_y)
    lax.fori_loop(marks[2], marks[3], attend, 0)
    before_y, _, _, _ = collect(copy_y, yr_s, y, NY)
    entering = faded_x[0:1] * before_y + before_x

    mine_half = pl.ds(pl.multiple_of(c * HALF, 8), HALF)
    other_half = pl.ds(pl.multiple_of((1 - c) * HALF, 8), HALF)

    def back(other, slot):
        return pltpu.make_async_remote_copy(
            src_ref=cs_s.at[other], dst_ref=carry_s.at[slot, mine_half, :], send_sem=b_ss.at[other], recv_sem=b_rs.at[slot],
            device_id=at_z(other), device_id_type=MESH,
        )

    def give(i, _):
        other = head_of(i)
        value = gp_s[other, 0:1, :] * entering + w_s[other]
        cs_s[other] = value
        back(other, z).start()
        return 0

    def forward(h):
        return pltpu.make_async_remote_copy(
            src_ref=carry_s.at[h, mine_half, :], dst_ref=carry_s.at[h, mine_half, :], send_sem=f_ss.at[h], recv_sem=f_rs.at[h],
            device_id=partner, device_id_type=MESH,
        )

    def forwarded(h):
        return pltpu.make_async_remote_copy(
            src_ref=carry_s.at[h, other_half, :], dst_ref=carry_s.at[h, other_half, :], send_sem=f_ss.at[h], recv_sem=f_rs.at[h],
            device_id=partner, device_id_type=MESH,
        )

    lax.fori_loop(0, NZ - 1, give, 0)
    carry_s[z, mine_half, :] = gp_s[z, 0:1, :] * entering + w_s[z]
    forward(z).start()
    lax.fori_loop(marks[3], marks[4], attend, 0)

    gain_copy.wait()

    def store(h):
        return pltpu.make_async_copy(o_s.at[h], out_hbm.at[:, columns(h)], o_sem.at[h])

    def pass_on(i):
        h = head_of(i)
        back(h, h).wait_recv()
        forward(h).start()

    def finish(i):
        h = head_of(i)
        forwarded(h).wait_recv()
        carry = carry_s[h]
        carry = jnp.where(c == 0, carry, peer_s[h, 0:1, :] * carry + peer_s[h, 8:MSG, :])
        gain = gain_s[h]
        col_e = pltpu.roll(cols_s[2], (HD - h) % HD, 1)
        for b in range(blocks):
            if b:
                carry = e_s[h, b - 1 : b, :] * carry
                start = carry + sblk_s[h, b - 1]
            else:
                start = carry
            high = start.astype(BF16)
            low = (start - high.astype(F32)).astype(BF16)
            both = jnp.concatenate([high, low], axis=0)
            place = slice(b * BLOCK, (b + 1) * BLOCK)
            query = q_s[h, place, :]
            through = jnp.dot(jnp.concatenate([query, query], axis=1), both, preferred_element_type=F32)
            for a in range(tiles):
                j = b * tiles + a
                here = slice(j * TILE, (j + 1) * TILE)
                value = y_s[h, here, :] + col_e[:, j * HEADS : j * HEADS + 1] * through[a * TILE : (a + 1) * TILE]
                scale = lax.rsqrt(jnp.mean(value * value, axis=-1, keepdims=True) + 1e-06)
                o_s[h, here, :] = (value * scale * gain).astype(BF16)
        store(h).start()

    def outputs(n, _):
        pass_on(HEADS - 1 - n - 1)
        finish(HEADS - 1 - n)
        return 0

    lax.fori_loop(0, HEADS - 1, outputs, 0)
    finish(0)

    def drain(h, _):
        to_partner(h).wait_send()
        forward(h).wait_send()
        store(h).wait()

        @pl.when(h != z)
        def _():
            to_owner(h).wait_send()
            back(h, z).wait_send()

        return 0

    lax.fori_loop(0, HEADS, drain, 0)
    for d in range(1, NX):
        copy_x(d, True).wait_send()
    for d in range(1, NY):
        copy_y(d, True).wait_send()


def shards(queries, keys, values, log_decay, gain):
    tokens = queries.shape[0]
    blocks = tokens // BLOCK
    heads = (HEADS, tokens, HD)
    vmem, dma = pltpu.VMEM, pltpu.SemaphoreType.DMA
    scratch = [
        vmem(heads, BF16), vmem(heads, BF16), vmem(heads, BF16),
        vmem((HEADS, tokens), F32), vmem((HEADS, 1, HD), F32),
        vmem((HEADS, 5, tokens), F32), vmem((3, TILE, TILE), F32), vmem((HEADS, blocks + 1, HD), F32),
        vmem((HEADS, blocks - 1, HD, HD), F32), vmem(heads, F32), vmem(heads, BF16),
        vmem((HEADS, MSG, HD), F32), vmem((HEADS, MSG, HD), F32),
        vmem((NZ, SLAB, HD), F32), vmem((NZ, SLAB, HD), F32),
        vmem((NZ, HALF, HD), F32), vmem((NZ, 8, HD), F32),
        vmem((SLAB, HD), F32), vmem((NX, SLAB, HD), F32),
        vmem((SLAB, HD), F32), vmem((NY, SLAB, HD), F32),
        vmem((NZ, HALF, HD), F32), vmem((HEADS, HD, HD), F32),
        dma((HEADS,)), dma((HEADS,)), dma((HEADS,)), dma((HEADS,)), dma((2,)),
        dma((HEADS,)), dma((HEADS,)), dma((NZ,)), dma((NZ,)),
        dma((NX - 1,)), dma((NX - 1,)), dma((NY - 1,)), dma((NY - 1,)),
        dma((NZ,)), dma((NZ,)), dma((HEADS,)), dma((HEADS,)),
    ]
    return pl.pallas_call(
        kernel,
        out_shape=jax.ShapeDtypeStruct(queries.shape, BF16),
        in_specs=[pl.BlockSpec(memory_space=pl.ANY)] * 5,
        out_specs=pl.BlockSpec(memory_space=pl.ANY),
        scratch_shapes=scratch,
        compiler_params=pltpu.CompilerParams(
            collective_id=0, has_side_effects=True, vmem_limit_bytes=48 * 1024 * 1024
        ),
        cost_estimate=pl.CostEstimate(flops=4 * 10**9, bytes_accessed=13 * 10**6, transcendentals=2 * 10**6),
    )(queries, keys, values, log_decay, gain.reshape(HEADS, 1, HD))


def solution(mesh):
    in_specs = (
        P(("seg", "ctx"), None),
        P(("seg", "ctx"), None),
        P(("seg", "ctx"), None),
        P(None, ("seg", "ctx")),
        P(),
    )
    out_specs = P(("seg", "ctx"), None)
    return jax.shard_map(shards, mesh=mesh, in_specs=in_specs, out_specs=out_specs, check_vma=False)
```

time: 400 us -> 54.8 us (0.14)
  the two profiles are of different devices: /device:TPU:9 before, /device:TPU:1 now
where the time goes in v1:
time: 54.8 us; the launch traced here: 54.6 us
  Pallas kernels  51.5 us (94%)
  local copies, waits for them, and re-layouts  3.15 us (6%)
    pallas_call x1, Pallas kernels, shards(): pl.pallas_call(kernel, out_shape=jax.ShapeDtypeStruct(queries.shape, BF16...  51.5 us
    unnamed x5, local copies, waits for them, and re-layouts  3.15 us

profile of v1, /device:TPU:1, one launch (start us, length us, event | category | flops | bytes accessed | tf_op | source)
XLA Modules:
  0.0 54.6 jit_solution(12116713074818227293)
XLA Ops:
  0.0 0.0 copy-start
  0.0 0.8 %copy-done = f32[8,1536]{1,0:T(8,128)S(1)} copy-done((f32[8,1536]{1,0:T(8,128)S(1)}, f32[8,1536]{1,0:T(8,128)}, u32[]{:S(2)}) %copy-start) | copy-done | bytes 49176
  0.8 0.0 copy-start.1
  0.8 0.7 %copy-done.1 = f32[1024]{0:T(1024)S(1)} copy-done((f32[1024]{0:T(1024)S(1)}, f32[1024]{0:T(1024)}, u32[]{:S(2)}) %copy-start.1) | copy-done | bytes 4120
  1.5 51.5 %shard_map.55 = bf16[1536,1024]{1,0:T(8,128)(2,1)S(1)} custom-call(bf16[1536,1024]{1,0:T(8,128)(2,1)} %q_hbm.1, bf16[1536,1024]{1,0:T(8,128)(2,1)} %k_hbm.1, bf16[1536,1024]{1,0:T(8,128)(2,1)} %v_hbm.1, f32[8,1536]{1,0:T(8,128)S(1)} %copy-done, f32[8,1,128]{2,1,0:T(1,128)S(1)} %bitcast.1), custom_call_target="tpu_custom_call" | custom-call | flops 4000000000 | bytes 13000000 | tf_op jit(solution)/shard_map/pallas_call | solution.py:398
  53.0 1.7 %copy.7 = bf16[1536,1024]{1,0:T(8,128)(2,1)} copy(bf16[1536,1024]{1,0:T(8,128)(2,1)S(1)} %shard_map.55) | data formatting | bytes 6291456
Async XLA Ops:
  0.0 0.8 %copy-start = (f32[8,1536]{1,0:T(8,128)S(1)}, f32[8,1536]{1,0:T(8,128)}, u32[]{:S(2)}) copy-start(f32[8,1536]{1,0:T(8,128)} %ld_hbm.1) | copy-start | bytes 147460
  0.8 0.7 %copy-start.1 = (f32[1024]{0:T(1024)S(1)}, f32[1024]{0:T(1024)}, u32[]{:S(2)}) copy-start(f32[1024]{0:T(1024)} %param.9) | copy-start | bytes 12292

commit v2 on v1

v2 whole, which is shorter than its diff:
```python
import jax
import jax.numpy as jnp
from jax import lax
from jax.experimental import pallas as pl
from jax.experimental.pallas import tpu as pltpu
from jax.sharding import PartitionSpec as P

HEADS = 8
HD = 128
BLOCK = 512
TILE = 128
NSEG, NZ = 16, 8
HALF = HD // 2
EARLY = 4
SLAB = HALF + 8
MSG = HD + 8
LOG2E = 1.4426950408889634
MESH = pl.DeviceIdType.MESH
F32, BF16 = jnp.float32, jnp.bfloat16
SPLIT = (3, 2, 3)


def order(i):
    return 4 + ((i + 1) // 2) * (1 - 2 * (i % 2))


def kernel(
    q_hbm, k_hbm, v_hbm, ld_hbm, gain_hbm, out_hbm,
    q_s, k_s, v_s, ld_s, gain_s, rows_s, cols_s, e_s, sblk_s, y_s, r_s, o_s,
    msg_s, peer_s, zs_s, zr_s, w_s, gp_s, t_s, got_s, cs_s, carry_s,
    q_sem, k_sem, v_sem, o_sem, small_sem,
    core_ss, core_rs, z_ss, z_rs, t_ss, t_rs, b_ss, b_rs, f_ss, f_rs, ready_sem,
):
    seg, ctx = lax.axis_index("seg"), lax.axis_index("ctx")
    z, c = ctx // 2, ctx % 2
    tokens = k_s.shape[1]
    blocks = tokens // BLOCK
    tiles = BLOCK // TILE

    def head_of(i):
        return (z + order(i)) % NZ

    def columns(h):
        return pl.ds(pl.multiple_of(h * HD, HD), HD)

    def at_z(other):
        return (seg, other * 2 + c)

    def at_seg(other):
        return (other, ctx)

    partner = (seg, z * 2 + (1 - c))

    barrier = pltpu.get_barrier_semaphore()

    def signal(device):
        pl.semaphore_signal(barrier, inc=1, device_id=device, device_id_type=MESH)

    for i in range(NZ - 1):
        signal(at_z(head_of(i)))
    signal(partner)
    ld_copy = pltpu.make_async_copy(ld_hbm, ld_s, small_sem.at[0])
    gain_copy = pltpu.make_async_copy(gain_hbm, gain_s, small_sem.at[1])
    ld_copy.start()

    def load(hbm, vmem, sem, h):
        return pltpu.make_async_copy(hbm.at[:, columns(h)], vmem.at[h], sem.at[h])

    def start_kv(i, _):
        h = head_of(i)
        load(k_hbm, k_s, k_sem, h).start()
        load(v_hbm, v_s, v_sem, h).start()
        return 0

    lax.fori_loop(0, HEADS, start_kv, 0)
    gain_copy.start()

    def start_q(h, _):
        load(q_hbm, q_s, q_sem, h).start()
        return 0

    lax.fori_loop(0, HEADS, start_q, 0)

    def greet(other, _):
        signal(at_seg(other))
        return 0

    lax.fori_loop(seg + 1, NSEG, greet, 0)

    ld_copy.wait()
    count = tokens // TILE
    stacked = jnp.concatenate([ld_s[:, j * TILE : (j + 1) * TILE] for j in range(count)], axis=0) * LOG2E
    rows = lax.broadcasted_iota(jnp.int32, (TILE, TILE), 0)
    cols = lax.broadcasted_iota(jnp.int32, (TILE, TILE), 1)
    upto = (rows <= cols).astype(F32)
    within = jnp.dot(stacked, upto, precision=lax.Precision.HIGHEST, preferred_element_type=F32)
    within = [within[j * HEADS : (j + 1) * HEADS] for j in range(count)]
    col_c, col_r = [], []
    total = jnp.zeros((HEADS, 1), F32)
    for b in range(blocks):
        start = [jnp.zeros((HEADS, 1), F32)]
        cum = []
        for a in range(tiles):
            w = within[b * tiles + a]
            cum.append(w + start[a])
            start.append(start[a] + w[:, TILE - 1 : TILE])
            col_r.append(jnp.exp2(w))
        last = start[tiles]
        col_c += cum
        for a in range(tiles):
            place = slice((b * tiles + a) * TILE, (b * tiles + a + 1) * TILE)
            rows_s[:, 0, place] = cum[a]
            rows_s[:, 4, place] = jnp.exp2(last - cum[a])
            for m in range(a + 1, tiles):
                rows_s[:, m, place] = jnp.exp2(start[m] - cum[a])
        e_s[:, b, :] = jnp.broadcast_to(jnp.exp2(last), (HEADS, HD))
        total = total + last
    e_s[:, blocks, :] = jnp.broadcast_to(jnp.exp2(total), (HEADS, HD))
    blank = jnp.zeros((TILE - count * HEADS, TILE), F32)
    cols_s[0] = jnp.transpose(jnp.concatenate(col_c + [blank], axis=0))
    cols_s[1] = jnp.transpose(jnp.concatenate(col_r + [blank], axis=0))

    def to_partner(h):
        return pltpu.make_async_remote_copy(
            src_ref=msg_s.at[h], dst_ref=peer_s.at[h], send_sem=core_ss.at[h], recv_sem=core_rs.at[h],
            device_id=partner, device_id_type=MESH,
        )

    def to_owner(h):
        return pltpu.make_async_remote_copy(
            src_ref=zs_s.at[h], dst_ref=zr_s.at[z], send_sem=z_ss.at[h], recv_sem=z_rs.at[z],
            device_id=at_z(h), device_id_type=MESH,
        )

    def from_shard(other):
        return pltpu.make_async_remote_copy(
            src_ref=zs_s.at[other], dst_ref=zr_s.at[other], send_sem=z_ss.at[other], recv_sem=z_rs.at[other],
            device_id=at_z(other), device_id_type=MESH,
        )

    def own_state(i):
        h = head_of(i)
        load(k_hbm, k_s, k_sem, h).wait()
        load(v_hbm, v_s, v_sem, h).wait()
        state = None
        for b in range(blocks):
            place = slice(b * BLOCK, (b + 1) * BLOCK)
            turned = jnp.transpose(k_s[h, place, :]).astype(F32)
            decayed = (turned * rows_s[h, 4:5, place]).astype(BF16)
            added = jnp.dot(decayed, v_s[h, place, :], preferred_element_type=F32)
            if b:
                sblk_s[h, b - 1] = state
                state = e_s[h, b : b + 1, :] * state + added
            else:
                state = added
        msg_s[h, 0:8, :] = jnp.broadcast_to(e_s[h, blocks : blocks + 1, :], (8, HD))
        msg_s[h, 8:MSG, :] = state

    def pair_state(i):
        h = head_of(i)
        to_partner(h).wait_recv()
        mine, other = msg_s[h, 0:8, :], peer_s[h, 0:8, :]
        half = pl.ds(pl.multiple_of(8 + c * HALF, 8), HALF)
        first = c == 0
        scale_mine = jnp.where(first, other, 1.0)[0:1]
        scale_other = jnp.where(first, 1.0, mine)[0:1]
        joined = scale_mine * msg_s[h, half, :] + scale_other * peer_s[h, half, :]
        zs_s[h, 0:8, :] = mine * other
        zs_s[h, 8:SLAB, :] = joined

        @pl.when(h != z)
        def _():
            to_owner(h).start()

        @pl.when(h == z)
        def _():
            zr_s[z, 0:8, :] = mine * other
            zr_s[z, 8:SLAB, :] = joined

    def states(i, _):
        own_state(i)
        return 0

    def send_states(i, _):
        to_partner(head_of(i)).start()
        return 0

    def joint(i, _):
        pair_state(i - EARLY)
        own_state(i)
        to_partner(head_of(i)).start()
        return 0

    def pair_states(i, _):
        pair_state(i)
        return 0

    def ready(other, _):
        pl.semaphore_signal(ready_sem, inc=1, device_id=at_seg(other), device_id_type=MESH)
        return 0

    lax.fori_loop(0, EARLY, states, 0)
    pl.semaphore_wait(barrier, 1 + (NZ - 1) + seg)
    lax.fori_loop(0, EARLY, send_states, 0)
    lax.fori_loop(EARLY, HEADS, joint, 0)
    lax.fori_loop(HEADS - EARLY, HEADS, pair_states, 0)
    lax.fori_loop(0, seg, ready, 0)

    below = cols <= rows

    def attend(h, _):
        load(q_hbm, q_s, q_sem, h).wait()
        shift = (HD - h) % HD
        col_c = pltpu.roll(cols_s[0], shift, 1)
        col_r = pltpu.roll(cols_s[1], shift, 1)
        for b in range(blocks):
            for a in range(tiles):
                j = b * tiles + a
                here = slice(j * TILE, (j + 1) * TILE)
                query = q_s[h, here, :]
                cum = jnp.broadcast_to(col_c[:, j * HEADS : j * HEADS + 1], (TILE, TILE))
                r_s[h, here, :] = jnp.exp2(cum)
                if a:
                    fade = jnp.broadcast_to(col_r[:, j * HEADS : j * HEADS + 1], (TILE, TILE))
                sums = None
                for first in range(0, a + 1, 2):
                    seen = range(first, min(first + 2, a + 1))
                    piece = slice((b * tiles + first) * TILE, (b * tiles + seen[-1] + 1) * TILE)
                    scores = lax.dot_general(
                        query, k_s[h, piece, :], (((1,), (1,)), ((), ())), preferred_element_type=F32
                    )
                    weights = []
                    for n, m in enumerate(seen):
                        score = scores[:, n * TILE : (n + 1) * TILE]
                        there = slice((b * tiles + m) * TILE, (b * tiles + m + 1) * TILE)
                        if m < a:
                            score = score * rows_s[h, a : a + 1, there] * fade
                        else:
                            score = score * jnp.where(below, jnp.exp2(cum - rows_s[h, 0:1, there]), 0.0)
                        weights.append(score.astype(BF16))
                    if len(weights) > 1:
                        weights = [jnp.concatenate(weights, axis=1)]
                    part = jnp.dot(weights[0], v_s[h, piece, :], preferred_element_type=F32)
                    sums = part if sums is None else sums + part
                y_s[h, here, :] = sums
        return 0

    marks = [0]
    for n in SPLIT:
        marks.append(marks[-1] + n)
    lax.fori_loop(marks[0], marks[1], attend, 0)

    def fold(n, held):
        state, decay = held

        @pl.when(n != z)
        def _():
            from_shard(n).wait_recv()

        w_s[n] = state
        gp_s[n] = decay
        g = zr_s[n, 0:8, :]
        return (g[0:1] * state + zr_s[n, 8:SLAB, :], decay * g)

    empty = (jnp.zeros((HALF, HD), F32), jnp.ones((8, HD), F32))
    state, decay = lax.fori_loop(0, NZ, fold, empty)
    t_s[0:8, :] = decay
    t_s[8:SLAB, :] = state

    def to_seg(other):
        return pltpu.make_async_remote_copy(
            src_ref=t_s, dst_ref=got_s.at[seg], send_sem=t_ss.at[other], recv_sem=t_rs.at[seg],
            device_id=at_seg(other), device_id_type=MESH,
        )

    def from_seg(other):
        return pltpu.make_async_remote_copy(
            src_ref=t_s, dst_ref=got_s.at[other], send_sem=t_ss.at[other], recv_sem=t_rs.at[other],
            device_id=at_seg(other), device_id_type=MESH,
        )

    def tell(n, _):
        to_seg(NSEG - 1 - n).start()
        return 0

    @pl.when(seg < NSEG - 1)
    def _():
        pl.semaphore_wait(ready_sem, NSEG - 1 - seg)

    lax.fori_loop(0, NSEG - 1 - seg, tell, 0)
    lax.fori_loop(marks[1], marks[2], attend, 0)

    def gather(n, entering):
        from_seg(n).wait_recv()
        return got_s[n, 0:1, :] * entering + got_s[n, 8:SLAB, :]

    entering = lax.fori_loop(0, seg, gather, jnp.zeros((HALF, HD), F32))

    mine_half = pl.ds(pl.multiple_of(c * HALF, 8), HALF)
    other_half = pl.ds(pl.multiple_of((1 - c) * HALF, 8), HALF)

    def back(other, slot):
        return pltpu.make_async_remote_copy(
            src_ref=cs_s.at[other], dst_ref=carry_s.at[slot, mine_half, :], send_sem=b_ss.at[other], recv_sem=b_rs.at[slot],
            device_id=at_z(other), device_id_type=MESH,
        )

    def give(n, _):
        other = lax.rem(n + jnp.where(n >= z, 1, 0), NZ)
        value = gp_s[other, 0:1, :] * entering + w_s[other]
        cs_s[other] = value
        back(other, z).start()
        return 0

    def forward(h):
        return pltpu.make_async_remote_copy(
            src_ref=carry_s.at[h, mine_half, :], dst_ref=carry_s.at[h, mine_half, :], send_sem=f_ss.at[h], recv_sem=f_rs.at[h],
            device_id=partner, device_id_type=MESH,
        )

    def forwarded(h):
        return pltpu.make_async_remote_copy(
            src_ref=carry_s.at[h, other_half, :], dst_ref=carry_s.at[h, other_half, :], send_sem=f_ss.at[h], recv_sem=f_rs.at[h],
            device_id=partner, device_id_type=MESH,
        )

    lax.fori_loop(0, NZ - 1, give, 0)
    carry_s[z, mine_half, :] = gp_s[z, 0:1, :] * entering + w_s[z]
    forward(z).start()
    lax.fori_loop(marks[2], marks[3], attend, 0)

    gain_copy.wait()

    def store(h):
        return pltpu.make_async_copy(o_s.at[h], out_hbm.at[:, columns(h)], o_sem.at[h])

    def pass_on(i):
        h = head_of(i)
        back(h, h).wait_recv()
        forward(h).start()

    def finish(i):
        h = head_of(i)
        forwarded(h).wait_recv()
        carry = carry_s[h]
        carry = jnp.where(c == 0, carry, peer_s[h, 0:1, :] * carry + peer_s[h, 8:MSG, :])
        gain = gain_s[h]
        for b in range(blocks):
            if b:
                carry = e_s[h, b - 1 : b, :] * carry
                start = carry + sblk_s[h, b - 1]
            else:
                start = carry
            high = start.astype(BF16)
            low = (start - high.astype(F32)).astype(BF16)
            both = jnp.concatenate([high, low], axis=0)
            for a in range(tiles):
                j = b * tiles + a
                here = slice(j * TILE, (j + 1) * TILE)
                query = q_s[h, here, :]
                through = jnp.dot(jnp.concatenate([query, query], axis=1), both, preferred_element_type=F32)
                value = y_s[h, here, :] + r_s[h, here, :] * through
                scale = lax.rsqrt(jnp.mean(value * value, axis=-1, keepdims=True) + 1e-06)
                o_s[h, here, :] = (value * scale * gain).astype(BF16)
        store(h).start()

    def outputs(n, _):
        pass_on(HEADS - 3 - n)
        finish(HEADS - 1 - n)
        return 0

    pass_on(HEADS - 2)
    lax.fori_loop(0, HEADS - 2, outputs, 0)

    def last_outputs(n, _):
        finish(1 - n)
        return 0

    lax.fori_loop(0, 2, last_outputs, 0)

    def drain(h, _):
        to_partner(h).wait_send()
        forward(h).wait_send()
        store(h).wait()

        @pl.when(h != z)
        def _():
            to_owner(h).wait_send()
            back(h, z).wait_send()

        return 0

    lax.fori_loop(0, HEADS, drain, 0)

    def drain_totals(other, _):
        to_seg(other).wait_send()
        return 0

    lax.fori_loop(seg + 1, NSEG, drain_totals, 0)


def shards(queries, keys, values, log_decay, gain):
    tokens = queries.shape[0]
    blocks = tokens // BLOCK
    heads = (HEADS, tokens, HD)
    vmem, dma = pltpu.VMEM, pltpu.SemaphoreType.DMA
    scratch = [
        vmem(heads, BF16), vmem(heads, BF16), vmem(heads, BF16),
        vmem((HEADS, tokens), F32), vmem((HEADS, 1, HD), F32),
        vmem((HEADS, 5, tokens), F32), vmem((2, TILE, TILE), F32), vmem((HEADS, blocks + 1, HD), F32),
        vmem((HEADS, blocks - 1, HD, HD), F32), vmem(heads, F32), vmem(heads, F32), vmem(heads, BF16),
        vmem((HEADS, MSG, HD), F32), vmem((HEADS, MSG, HD), F32),
        vmem((NZ, SLAB, HD), F32), vmem((NZ, SLAB, HD), F32),
        vmem((NZ, HALF, HD), F32), vmem((NZ, 8, HD), F32),
        vmem((SLAB, HD), F32), vmem((NSEG, SLAB, HD), F32),
        vmem((NZ, HALF, HD), F32), vmem((HEADS, HD, HD), F32),
        dma((HEADS,)), dma((HEADS,)), dma((HEADS,)), dma((HEADS,)), dma((2,)),
        dma((HEADS,)), dma((HEADS,)), dma((NZ,)), dma((NZ,)),
        dma((NSEG,)), dma((NSEG,)), dma((NZ,)), dma((NZ,)), dma((HEADS,)), dma((HEADS,)),
        pltpu.SemaphoreType.REGULAR,
    ]
    operands = (queries, keys, values, log_decay, gain.reshape(HEADS, 1, HD))
    operands = [pltpu.with_memory_space_constraint(a, pltpu.HBM) for a in operands]
    return pl.pallas_call(
        kernel,
        out_shape=jax.ShapeDtypeStruct(queries.shape, BF16),
        in_specs=[pl.BlockSpec(memory_space=pltpu.HBM)] * 5,
        out_specs=pl.BlockSpec(memory_space=pl.ANY),
        scratch_shapes=scratch,
        compiler_params=pltpu.CompilerParams(
            collective_id=0, has_side_effects=True, vmem_limit_bytes=48 * 1024 * 1024
        ),
        cost_estimate=pl.CostEstimate(flops=4 * 10**9, bytes_accessed=13 * 10**6, transcendentals=2 * 10**6),
    )(*operands)


def solution(mesh):
    in_specs = (
        P(("seg", "ctx"), None),
        P(("seg", "ctx"), None),
        P(("seg", "ctx"), None),
        P(None, ("seg", "ctx")),
        P(),
    )
    out_specs = P(("seg", "ctx"), None)
    return jax.shard_map(shards, mesh=mesh, in_specs=in_specs, out_specs=out_specs, check_vma=False)
```

time: 54.8 us -> 40.5 us (0.74)
  the two profiles are of different devices: /device:TPU:1 before, /device:TPU:9 now
where the time goes in v2:
time: 40.5 us; the launch traced here: 40.4 us
  Pallas kernels  38.7 us (96%)
  local copies, waits for them, and re-layouts  1.67 us (4%)
    pallas_call x1, Pallas kernels, shards(): pl.pallas_call(kernel, out_shape=jax.ShapeDtypeStruct(queries.shape, BF16...  38.7 us
    unnamed x1, local copies, waits for them, and re-layouts  1.67 us

profile of v2, /device:TPU:9, one launch (start us, length us, event | category | flops | bytes accessed | tf_op | source)
XLA Modules:
  0.0 40.4 jit_solution(793896539233765367)
XLA Ops:
  0.0 38.7 %shard_map.55 = bf16[1536,1024]{1,0:T(8,128)(2,1)S(1)} custom-call(bf16[1536,1024]{1,0:T(8,128)(2,1)} %q_hbm.1, bf16[1536,1024]{1,0:T(8,128)(2,1)} %k_hbm.1, bf16[1536,1024]{1,0:T(8,128)(2,1)} %v_hbm.1, f32[8,1536]{1,0:T(8,128)} %ld_hbm.1, f32[8,1,128]{2,1,0:T(1,128)} %bitcast.1), custom_call_target="tpu_custom_call" | custom-call | flops 4000000000 | bytes 13000000 | tf_op jit(solution)/shard_map/pallas_call | solution.py:424
  38.7 1.7 %copy.7 = bf16[1536,1024]{1,0:T(8,128)(2,1)} copy(bf16[1536,1024]{1,0:T(8,128)(2,1)S(1)} %shard_map.55) | data formatting | bytes 6291456

commit v3 on v2

--- a/solution.py
+++ b/solution.py
@@ -11,13 +11,13 @@
 TILE = 128
 NSEG, NZ = 16, 8
 HALF = HD // 2
-EARLY = 4
+EARLY = 8
 SLAB = HALF + 8
 MSG = HD + 8
 LOG2E = 1.4426950408889634
 MESH = pl.DeviceIdType.MESH
 F32, BF16 = jnp.float32, jnp.bfloat16
-SPLIT = (3, 2, 3)
+SPLIT = (3, 3, 2)
 
 
 def order(i):
@@ -56,12 +56,10 @@
     def signal(device):
         pl.semaphore_signal(barrier, inc=1, device_id=device, device_id_type=MESH)
 
-    for i in range(NZ - 1):
-        signal(at_z(head_of(i)))
-    signal(partner)
     ld_copy = pltpu.make_async_copy(ld_hbm, ld_s, small_sem.at[0])
     gain_copy = pltpu.make_async_copy(gain_hbm, gain_s, small_sem.at[1])
     ld_copy.start()
+    gain_copy.start()
 
     def load(hbm, vmem, sem, h):
         return pltpu.make_async_copy(hbm.at[:, columns(h)], vmem.at[h], sem.at[h])
@@ -73,19 +71,32 @@
         return 0
 
     lax.fori_loop(0, HEADS, start_kv, 0)
-    gain_copy.start()
 
     def start_q(h, _):
         load(q_hbm, q_s, q_sem, h).start()
         return 0
 
-    lax.fori_loop(0, HEADS, start_q, 0)
-
-    def greet(other, _):
+    def greet_z(other, _):
+        signal(at_z(other))
+        return 0
+
+    def greet_seg(other, _):
         signal(at_seg(other))
         return 0
 
-    lax.fori_loop(seg + 1, NSEG, greet, 0)
+    def ready_z(other, _):
+        pl.semaphore_signal(ready_sem.at[0], inc=1, device_id=at_z(other), device_id_type=MESH)
+        return 0
+
+    def ready_seg(other, _):
+        pl.semaphore_signal(ready_sem.at[1], inc=1, device_id=at_seg(other), device_id_type=MESH)
+        return 0
+
+    signal(partner)
+    lax.fori_loop(z + 1, NZ, greet_z, 0)
+    lax.fori_loop(seg + 1, NSEG, greet_seg, 0)
+    pl.semaphore_wait(barrier, 1 + z + seg)
+    lax.fori_loop(0, z, ready_z, 0)
 
     ld_copy.wait()
     count = tokens // TILE
@@ -179,9 +190,6 @@
 
     def states(i, _):
         own_state(i)
-        return 0
-
-    def send_states(i, _):
         to_partner(head_of(i)).start()
         return 0
 
@@ -195,16 +203,16 @@
         pair_state(i)
         return 0
 
-    def ready(other, _):
-        pl.semaphore_signal(ready_sem, inc=1, device_id=at_seg(other), device_id_type=MESH)
-        return 0
-
     lax.fori_loop(0, EARLY, states, 0)
-    pl.semaphore_wait(barrier, 1 + (NZ - 1) + seg)
-    lax.fori_loop(0, EARLY, send_states, 0)
+
+    @pl.when(z < NZ - 1)
+    def _():
+        pl.semaphore_wait(ready_sem.at[0], NZ - 1 - z)
+
     lax.fori_loop(EARLY, HEADS, joint, 0)
+    lax.fori_loop(0, HEADS, start_q, 0)
     lax.fori_loop(HEADS - EARLY, HEADS, pair_states, 0)
-    lax.fori_loop(0, seg, ready, 0)
+    lax.fori_loop(0, seg, ready_seg, 0)
 
     below = cols <= rows
 
@@ -285,7 +293,7 @@
 
     @pl.when(seg < NSEG - 1)
     def _():
-        pl.semaphore_wait(ready_sem, NSEG - 1 - seg)
+        pl.semaphore_wait(ready_sem.at[1], NSEG - 1 - seg)
 
     lax.fori_loop(0, NSEG - 1 - seg, tell, 0)
     lax.fori_loop(marks[1], marks[2], attend, 0)
@@ -417,7 +425,7 @@
         dma((HEADS,)), dma((HEADS,)), dma((HEADS,)), dma((HEADS,)), dma((2,)),
         dma((HEADS,)), dma((HEADS,)), dma((NZ,)), dma((NZ,)),
         dma((NSEG,)), dma((NSEG,)), dma((NZ,)), dma((NZ,)), dma((HEADS,)), dma((HEADS,)),
-        pltpu.SemaphoreType.REGULAR,
+        pltpu.SemaphoreType.REGULAR((2,)),
     ]
     operands = (queries, keys, values, log_decay, gain.reshape(HEADS, 1, HD))
     operands = [pltpu.with_memory_space_constraint(a, pltpu.HBM) for a in operands]

time: 40.5 us -> 39.6 us (0.978)
  Pallas kernels: 38.7 us -> 37.8 us
    pallas_call x1, Pallas kernels: 38.7 us -> 37.8 us  [shards(): pl.pallas_call(kernel, out_shape=jax.ShapeDtypeStruct(queries.shape, BF16...]
where the time goes in v3:
time: 39.6 us; the launch traced here: 39.5 us
  Pallas kernels  37.8 us (95%)
  local copies, waits for them, and re-layouts  1.67 us (4%)
    pallas_call x1, Pallas kernels, shards(): pl.pallas_call(kernel, out_shape=jax.ShapeDtypeStruct(queries.shape, BF16...  37.8 us
    unnamed x1, local copies, waits for them, and re-layouts  1.67 us

profile of v3, /device:TPU:9, one launch (start us, length us, event | category | flops | bytes accessed | tf_op | source)
XLA Modules:
  0.0 39.5 jit_solution(14790291848764863296)
XLA Ops:
  0.0 37.8 %shard_map.55 = bf16[1536,1024]{1,0:T(8,128)(2,1)S(1)} custom-call(bf16[1536,1024]{1,0:T(8,128)(2,1)} %q_hbm.1, bf16[1536,1024]{1,0:T(8,128)(2,1)} %k_hbm.1, bf16[1536,1024]{1,0:T(8,128)(2,1)} %v_hbm.1, f32[8,1536]{1,0:T(8,128)} %ld_hbm.1, f32[8,1,128]{2,1,0:T(1,128)} %bitcast.1), custom_call_target="tpu_custom_call" | custom-call | flops 4000000000 | bytes 13000000 | tf_op jit(solution)/shard_map/pallas_call | solution.py:432
  37.8 1.7 %copy.7 = bf16[1536,1024]{1,0:T(8,128)(2,1)} copy(bf16[1536,1024]{1,0:T(8,128)(2,1)S(1)} %shard_map.55) | data formatting | bytes 6291456

commit v4 on v3

--- a/solution.py
+++ b/solution.py
@@ -25,10 +25,10 @@
 
 
 def kernel(
-    q_hbm, k_hbm, v_hbm, ld_hbm, gain_hbm, out_hbm,
-    q_s, k_s, v_s, ld_s, gain_s, rows_s, cols_s, e_s, sblk_s, y_s, r_s, o_s,
+    q_hbm, k_hbm, v_hbm, ld_hbm, gain_hbm, out,
+    q_s, k_s, v_s, ld_s, gain_s, rows_s, cols_s, e_s, sblk_s, y_s, r_s,
     msg_s, peer_s, zs_s, zr_s, w_s, gp_s, t_s, got_s, cs_s, carry_s,
-    q_sem, k_sem, v_sem, o_sem, small_sem,
+    q_sem, k_sem, v_sem, small_sem,
     core_ss, core_rs, z_ss, z_rs, t_ss, t_rs, b_ss, b_rs, f_ss, f_rs, ready_sem,
 ):
     seg, ctx = lax.axis_index("seg"), lax.axis_index("ctx")
@@ -339,9 +339,6 @@
 
     gain_copy.wait()
 
-    def store(h):
-        return pltpu.make_async_copy(o_s.at[h], out_hbm.at[:, columns(h)], o_sem.at[h])
-
     def pass_on(i):
         h = head_of(i)
         back(h, h).wait_recv()
@@ -369,8 +366,7 @@
                 through = jnp.dot(jnp.concatenate([query, query], axis=1), both, preferred_element_type=F32)
                 value = y_s[h, here, :] + r_s[h, here, :] * through
                 scale = lax.rsqrt(jnp.mean(value * value, axis=-1, keepdims=True) + 1e-06)
-                o_s[h, here, :] = (value * scale * gain).astype(BF16)
-        store(h).start()
+                out[here, columns(h)] = (value * scale * gain).astype(BF16)
 
     def outputs(n, _):
         pass_on(HEADS - 3 - n)
@@ -389,7 +385,6 @@
     def drain(h, _):
         to_partner(h).wait_send()
         forward(h).wait_send()
-        store(h).wait()
 
         @pl.when(h != z)
         def _():
@@ -416,13 +411,13 @@
         vmem(heads, BF16), vmem(heads, BF16), vmem(heads, BF16),
         vmem((HEADS, tokens), F32), vmem((HEADS, 1, HD), F32),
         vmem((HEADS, 5, tokens), F32), vmem((2, TILE, TILE), F32), vmem((HEADS, blocks + 1, HD), F32),
-        vmem((HEADS, blocks - 1, HD, HD), F32), vmem(heads, F32), vmem(heads, F32), vmem(heads, BF16),
+        vmem((HEADS, blocks - 1, HD, HD), F32), vmem(heads, F32), vmem(heads, F32),
         vmem((HEADS, MSG, HD), F32), vmem((HEADS, MSG, HD), F32),
         vmem((NZ, SLAB, HD), F32), vmem((NZ, SLAB, HD), F32),
         vmem((NZ, HALF, HD), F32), vmem((NZ, 8, HD), F32),
         vmem((SLAB, HD), F32), vmem((NSEG, SLAB, HD), F32),
         vmem((NZ, HALF, HD), F32), vmem((HEADS, HD, HD), F32),
-        dma((HEADS,)), dma((HEADS,)), dma((HEADS,)), dma((HEADS,)), dma((2,)),
+        dma((HEADS,)), dma((HEADS,)), dma((HEADS,)), dma((2,)),
         dma((HEADS,)), dma((HEADS,)), dma((NZ,)), dma((NZ,)),
         dma((NSEG,)), dma((NSEG,)), dma((NZ,)), dma((NZ,)), dma((HEADS,)), dma((HEADS,)),
         pltpu.SemaphoreType.REGULAR((2,)),
@@ -433,7 +428,7 @@
         kernel,
         out_shape=jax.ShapeDtypeStruct(queries.shape, BF16),
         in_specs=[pl.BlockSpec(memory_space=pltpu.HBM)] * 5,
-        out_specs=pl.BlockSpec(memory_space=pl.ANY),
+        out_specs=pl.BlockSpec(memory_space=pltpu.VMEM),
         scratch_shapes=scratch,
         compiler_params=pltpu.CompilerParams(
             collective_id=0, has_side_effects=True, vmem_limit_bytes=48 * 1024 * 1024

time: 39.6 us -> 39 us (0.985)
  Pallas kernels: 37.8 us -> 37.2 us
    pallas_call x1, Pallas kernels: 37.8 us -> 37.2 us  [shards(): pl.pallas_call(kernel, out_shape=jax.ShapeDtypeStruct(queries.shape, BF16...]
where the time goes in v4:
time: 39 us; the launch traced here: 38.9 us
  Pallas kernels  37.2 us (95%)
  local copies, waits for them, and re-layouts  1.67 us (4%)
    pallas_call x1, Pallas kernels, shards(): pl.pallas_call(kernel, out_shape=jax.ShapeDtypeStruct(queries.shape, BF16...  37.2 us
    unnamed x1, local copies, waits for them, and re-layouts  1.67 us

profile of v4, /device:TPU:9, one launch (start us, length us, event | category | flops | bytes accessed | tf_op | source)
XLA Modules:
  0.0 38.9 jit_solution(11263345770830538635)
XLA Ops:
  0.0 37.2 %shard_map.55 = bf16[1536,1024]{1,0:T(8,128)(2,1)S(1)} custom-call(bf16[1536,1024]{1,0:T(8,128)(2,1)} %q_hbm.1, bf16[1536,1024]{1,0:T(8,128)(2,1)} %k_hbm.1, bf16[1536,1024]{1,0:T(8,128)(2,1)} %v_hbm.1, f32[8,1536]{1,0:T(8,128)} %ld_hbm.1, f32[8,1,128]{2,1,0:T(1,128)} %bitcast.1), custom_call_target="tpu_custom_call" | custom-call | flops 4000000000 | bytes 13000000 | tf_op jit(solution)/shard_map/pallas_call | solution.py:427
  37.2 1.7 %copy.7 = bf16[1536,1024]{1,0:T(8,128)(2,1)} copy(bf16[1536,1024]{1,0:T(8,128)(2,1)S(1)} %shard_map.55) | data formatting | bytes 6291456
